TPU v7x, 128 devices: a whole 4x4x4 slice. The times are simulated.
128 devices in a mesh: gx: 2 (over core), gy: 2 (over x_hi), gz: 32 (over z, y, x_lo).
Axes of the slice: x: 4 (x_hi: 2, x_lo: 2; x = x_hi * 2 + x_lo), y: 4, z: 4, core: 2. Of those that a mesh axis runs over, the one named last changes fastest.
Arguments:
- charges: bfloat16 [32, 48, 8192], P('gx', 'gy', 'gz'), may hold values from -6 to 6
- kernel_fine: bfloat16 [9, 9, 9], replicated, may hold values from -0.21875 to 0.21875
- kernel_mid: bfloat16 [9, 9, 9], replicated, may hold values from -0.21875 to 0.21875
- gauss_width: float32 [8], replicated, may hold values from 1 to 256
- gauss_weight: float32 [8], replicated, may hold values from 0.25 to 2
Outputs:
- potential: float32 [32, 48, 8192], P('gx', 'gy', 'gz')
All inputs are finite; a program needn't handle non-finite values.
Results may differ from a plain program's by a relative error of at most 0.002.
Values may be sent and summed in bfloat16 or wider, within the bound.
A program may use at most 384 MiB of HBM per device.

v0:
```python
import jax
import jax.numpy as jnp
from jax import lax
from jax.sharding import PartitionSpec as P

M = 16


def padded_2(cells, sides, width):
    for axis, dim in sides:
        count = lax.axis_size(axis)
        ends = count - 1
        head = lax.slice_in_dim(cells, 0, width, axis=dim)
        tail = lax.slice_in_dim(cells, cells.shape[dim] - width, cells.shape[dim], axis=dim)
        cells = jnp.concatenate(
            [
                lax.ppermute(tail, axis, [(i, (i + 1) % count) for i in range(ends)]),
                cells,
                lax.ppermute(head, axis, [((i + 1) % count, i) for i in range(ends)]),
            ],
            axis=dim,
        )
    return cells


def stencil(offset):
    value = jnp.zeros(offset.shape, jnp.float32)
    value = jnp.where(jnp.abs(offset) == 1, 9.0 / 16.0, value)
    value = jnp.where(offset == 0, 1.0, value)
    value = jnp.where(jnp.abs(offset) == 3, -1.0 / 16.0, value)
    return value


def restrict_band(rows, cols, margin):
    row_ids = jnp.arange(rows, dtype=jnp.int32)[:, None]
    col_ids = jnp.arange(cols, dtype=jnp.int32)[None, :]
    return stencil(col_ids - margin - 2 * row_ids)


def prolong_band(rows, cols):
    row_ids = jnp.arange(rows, dtype=jnp.int32)[:, None]
    col_ids = jnp.arange(cols, dtype=jnp.int32)[None, :]
    return stencil(row_ids - 2 * col_ids + 4)


def restrict_padded(padded, sizes, margin):
    highest = lax.Precision.HIGHEST
    band_x = restrict_band(sizes[0], padded.shape[0], margin).astype(jnp.bfloat16)
    band_y = restrict_band(sizes[1], padded.shape[1], margin)
    band_z = restrict_band(sizes[2], padded.shape[2], margin)
    field = jnp.einsum("ia,abcm->ibcm", band_x, padded, preferred_element_type=jnp.float32)
    field = jnp.einsum("jb,ibcm->ijcm", band_y, field, precision=highest)
    field = jnp.einsum("kc,ijcm->ijkm", band_z, field, precision=highest)
    return field


def prolong_ext(field, sizes):
    highest = lax.Precision.HIGHEST
    field = jnp.einsum(
        "ia,abcm->ibcm", prolong_band(sizes[0], field.shape[0]), field, precision=highest
    )
    field = jnp.einsum(
        "jb,ibcm->ijcm", prolong_band(sizes[1], field.shape[1]), field, precision=highest
    )
    field = jnp.einsum(
        "kc,ijcm->ijkm", prolong_band(sizes[2], field.shape[2]), field, precision=highest
    )
    return field


def correlate(padded, kernel, out_sizes):
    reach = jnp.arange(9, dtype=jnp.int32)[:, None, None]
    lag_y = (
        jnp.arange(padded.shape[1], dtype=jnp.int32)[:, None]
        - jnp.arange(out_sizes[1], dtype=jnp.int32)[None, :]
    )
    lag_z = (
        jnp.arange(padded.shape[2], dtype=jnp.int32)[:, None]
        - jnp.arange(out_sizes[2], dtype=jnp.int32)[None, :]
    )
    pick_y = (lag_y[None] == reach).astype(jnp.bfloat16)
    pick_z = (lag_z[None] == reach).astype(jnp.bfloat16)
    total = jnp.zeros((out_sizes[0], out_sizes[1], out_sizes[2], padded.shape[3]), jnp.float32)
    for offset in range(9):
        table = jnp.einsum(
            "bc,bpy,cqz->pqyz", kernel[offset], pick_y, pick_z, preferred_element_type=jnp.float32
        ).astype(jnp.bfloat16)
        total = total + jnp.einsum(
            "xpqm,pqyz->xyzm",
            padded[offset : offset + out_sizes[0]],
            table,
            preferred_element_type=jnp.float32,
        )
    return total


def gaussian_table(first_row, rows, cols, whole, gauss_width):
    row_pos = first_row + jnp.arange(rows, dtype=jnp.int32)
    col_pos = jnp.arange(cols, dtype=jnp.int32)
    spread = (row_pos[:, None] - col_pos[None, :]).astype(jnp.float32)
    width = gauss_width[:, None, None]
    table = jnp.exp(-jnp.square(spread[None] / width)) / jnp.sqrt(width)
    inside = (row_pos >= 0) & (row_pos < whole)
    return jnp.where(inside[None, :, None], table, 0.0)


def inside_mask(position, count, local, rim):
    spots = position * local - rim + jnp.arange(local + 2 * rim, dtype=jnp.int32)
    return ((spots >= 0) & (spots < local * count)).astype(jnp.float32)


def per_device(charges, kernel_fine, kernel_mid, gauss_width, gauss_weight):
    highest = lax.Precision.HIGHEST
    size_x, size_y, flat = charges.shape
    members = M
    size_z = flat // members
    field = charges.reshape(size_x, size_y, size_z, members)
    padded = padded_2(field, (("gx", 0), ("gy", 1), ("gz", 2)), 4)
    short_fine = correlate(padded, kernel_fine, (size_x, size_y, size_z))
    mid_sizes = (size_x // 2, size_y // 2, size_z // 2)
    q_mid = restrict_padded(padded, mid_sizes, 4).astype(jnp.bfloat16)
    mid_padded = padded_2(q_mid, (("gx", 0), ("gy", 1), ("gz", 2)), 6)
    short_mid = correlate(
        mid_padded, kernel_mid, (mid_sizes[0] + 4, mid_sizes[1] + 4, mid_sizes[2] + 4)
    )
    top_x, top_y, top_z = (size_x // 4, size_y // 4, size_z // 4)
    q_top = restrict_padded(mid_padded, (top_x, top_y, top_z), 6)
    count_x = lax.axis_size("gx")
    count_y = lax.axis_size("gy")
    count_z = lax.axis_size("gz")
    index_x = lax.axis_index("gx")
    index_y = lax.axis_index("gy")
    index_z = lax.axis_index("gz")
    whole_x = top_x * count_x
    whole_y = top_y * count_y
    whole_z = top_z * count_z
    first_x = index_x * top_x - 3
    first_y = index_y * top_y - 3
    first_z = index_z * top_z - 3
    scaled = gauss_weight[:, None, None]
    piece = lax.all_gather(q_top, "gx", axis=0, tiled=True)
    table = gaussian_table(first_x, top_x + 6, piece.shape[0], whole_x, gauss_width) * scaled
    section = jnp.einsum("gia,abcm->gibcm", table, piece, precision=highest)
    piece = lax.all_gather(section, "gy", axis=2, tiled=True)
    table = gaussian_table(first_y, top_y + 6, piece.shape[2], whole_y, gauss_width)
    section = jnp.einsum("gjb,gibcm->gijcm", table, piece, precision=highest)
    piece = lax.all_gather(section, "gz", axis=3, tiled=True)
    table = gaussian_table(first_z, top_z + 6, piece.shape[3], whole_z, gauss_width)
    section = jnp.einsum("gkc,gijcm->gijkm", table, piece, precision=highest)
    phi_top = jnp.sum(section, axis=0)
    ext_sizes = (mid_sizes[0] + 4, mid_sizes[1] + 4, mid_sizes[2] + 4)
    phi_mid = short_mid + prolong_ext(phi_top, ext_sizes)
    mask_x = inside_mask(index_x, count_x, mid_sizes[0], 2)
    mask_y = inside_mask(index_y, count_y, mid_sizes[1], 2)
    mask_z = inside_mask(index_z, count_z, mid_sizes[2], 2)
    phi_mid = (
        phi_mid
        * mask_x[:, None, None, None]
        * mask_y[None, :, None, None]
        * mask_z[None, None, :, None]
    )
    potential = short_fine + prolong_ext(phi_mid, (size_x, size_y, size_z))
    return potential.reshape(size_x, size_y, size_z * members)


def solution(mesh):
    placed = (P("gx", "gy", "gz"), P(), P(), P(), P())
    return jax.shard_map(
        per_device, mesh=mesh, in_specs=placed, out_specs=P("gx", "gy", "gz"), check_vma=False
    )
```

profile of v0, /device:TPU:1, one launch (start us, length us, event | category | flops | bytes accessed | tf_op | source)
XLA Modules:
  0.0 2214.8 jit_solution(8135780972543989800)
XLA Ops:
  9.0 3.4 collective-permute-start.1
  16.3 3.2 copy.19
  19.5 5.9 collective-permute-start.2
  30.6 3.9 copy.21
  34.5 5.2 collective-permute-done.3
  39.7 4.6 copy.22
  50.0 5.9 collective-permute-done.4
  56.0 11.3 collective-permute-done.5
  71.2 7.8 fusion.60
  79.1 7.4 fusion.212
  88.4 3.8 collective-permute-start.7
  96.0 3.7 collective-permute-done.8
  99.7 5.3 collective-permute-done.9
  111.2 7.0 collective-permute-done.10
  119.7 12.0 collective-permute-done.11
  133.2 5.7 pad_maximum_fusion
  138.9 6.0 copy.65
  147.0 4.7 convolution_bitcast_fusion.2
  152.0 3.8 all_gather.9
  157.4 37.8 %all_gather.10 = f32[8,10,12,4,16]{4,1,3,2,0:T(8,128)S(1)} all-gather(f32[8,10,6,4,16]{4,1,3,2,0:T(8,128)S(1)} %fusion.98), channel_id=1, replica_groups=mesh['gx'=2,'gy'=2,'gz'=32] {'gy'}, dimensions={2}, use_global_device_ids=true | all-gather | bytes 368640 | tf_op jit(solution)/shard_map/all_gather | solution.py:144
  195.2 6.8 fusion.33
  204.5 4.1 copy.116
  210.3 3.7 copy.120
  215.7 3.7 copy.124
  221.2 3.7 copy.128
  226.6 3.7 copy.132
  232.0 3.7 copy.136
  237.4 3.7 copy.140
  242.8 3.7 copy.144
  248.2 3.8 copy.112
  274.6 6.8 fusion.10
  281.4 4.8 fusion.12
  286.3 4.9 fusion.14
  291.2 4.9 fusion.16
  296.1 4.8 fusion.18
  300.9 5.4 fusion.6
  306.4 4.9 fusion.8
  311.3 4.9 fusion.4
  331.5 1624.0 %all-gather.2.cloned.1.call-done = f32[8,10,12,128,16]{2,4,3,1,0:T(8,128)} async-done(((f32[8,10,12,4,16]{2,4,3,1,0:T(8,128)}), f32[8,10,12,128,16]{2,4,3,1,0:T(8,128)}) %all-gather.2.cloned.1.call-update) | async-done | bytes 7864336 | tf_op jit(solution)/shard_map/all_gather | solution.py:147
  1955.5 98.0 %copy.70 = f32[8,10,12,128,16]{4,3,0,2,1:T(8,128)} copy(f32[8,10,12,128,16]{2,4,3,1,0:T(8,128)} %all-gather.2.cloned.1.call-done) | data formatting | bytes 15728640 | tf_op jit(solution)/shard_map/all_gather | solution.py:147
  2053.5 104.5 %convolution_bitcast_fusion.1 = f32[10,12,10,16]{2,3,1,0:T(8,128)} fusion(f32[8,10,12,128,16]{4,3,0,2,1:T(8,128)} %copy.70, f32[8]{0:T(128)S(1)} %sqrt.6, f32[8]{0:T(128)S(1)} %copy-done.26, f32[10,128]{1,0:T(8,128)S(1)} %subtract_convert_fusion, pred[10]{0:T(512)(128)(4,1)S(1)} %compare_and_fusion), kind=kOutput, calls=%fused_computation.106 | convolution fusion | flops 235980800 | bytes 7946314 | tf_op jit(solution)/shard_map/gkc,gijcm->gijkm/dot_general | solution.py:149
  2158.0 3.4 copy.71
  2163.5 3.0 convolution_bitcast_fusion
  2166.5 3.5 copy.73
  2170.1 3.9 fusion.176
  2174.0 3.9 copy.74
  2177.9 5.7 fusion.75
  2193.0 9.8 bitcast_add_fusion
  (165 shorter events, 110.1 us)
Async XLA Ops:
  6.5 1949.0 %all-gather.2.cloned.1.call-start = ((), (), s32[]{:S(2)}) async-start(), calls=%async_computation | async-start | bytes 86507520 | tf_op jit(solution)/shard_map/all_gather | solution.py:147
  7.5 6.4 collective-permute-start
  9.0 5.0 collective-permute-start.1
  12.4 58.8 %copy-start.24 = (s32[12]{0:T(128)}, s32[12]{0:T(128)S(1)}, u32[]{:S(2)}) copy-start(s32[12]{0:T(128)S(1)} %iota_multiply_fusion.5) | copy-start | bytes 148
  19.5 11.0 collective-permute-start.2
  28.3 11.5 collective-permute-start.3
  44.3 22.9 %copy-start = (bf16[24,4,16,16]{1,3,2,0:T(8,128)(2,1)S(1)}, bf16[24,4,16,16]{1,3,2,0:T(8,128)(2,1)}, u32[]{:S(2)}) copy-start(bf16[24,4,16,16]{1,3,2,0:T(8,128)(2,1)} %copy.22) | copy-start | bytes 147460
  46.3 9.6 collective-permute-start.4
  48.6 18.7 collective-permute-start.5
  69.4 9.6 copy-start.1
  79.1 16.9 copy-start.26
  87.1 5.1 collective-permute-start.6
  88.4 4.8 collective-permute-start.7
  93.3 6.4 collective-permute-start.8
  94.6 10.4 collective-permute-start.9
  99.7 5.3 copy-start.20
  105.0 0.7 copy-start.21
  106.9 11.3 collective-permute-start.10
  109.7 22.0 collective-permute-start.11
  144.9 10.9 copy-start.27
  202.0 0.8 copy-start.22
  246.5 7.5 copy-start.23
  274.6 6.8 copy-start.2
  274.6 6.8 copy-start.11
  281.4 4.8 copy-start.10
  286.3 4.9 copy-start.9
  291.2 4.9 copy-start.8
  296.1 4.8 copy-start.7
  300.9 5.5 copy-start.6
  306.4 4.9 copy-start.5
  311.3 4.9 copy-start.12
  316.1 1.9 copy-start.13
  318.0 1.9 copy-start.14
  319.9 1.9 copy-start.15
  321.9 1.9 copy-start.16
  323.8 1.9 copy-start.17
  325.7 1.9 copy-start.18
  327.6 2.0 copy-start.19
  2158.0 5.5 copy-start.25
  2174.0 3.9 copy-start.29
  2174.0 3.9 copy-start.30
  2174.0 3.9 copy-start.31
  2186.5 2.7 copy-start.28
  2189.2 3.8 copy-start.4
  2189.3 3.8 copy-start.32
  2191.1 1.9 copy-start.3
Sparse Core Ops, SparseCore 0:
  202.1 1753.3 all-gather.1
where the time goes:
time: 2220 us; the launch traced here: 2210 us
  waiting for transfers between devices  1680 us (76%)
  matrix products  261 us (12%)
  local copies, waits for them, and re-layouts  182 us (8%)
  blocking collectives  41.6 us (2%)
  starting transfers between devices  27 us (1%)
    all_gather x1, waiting for transfers between devices, per_device(): piece = lax.all_gather(section, 'gz', axis=3, tiled=True)  1620 us
    dot_general x1, matrix products, per_device(): section = jnp.einsum('gkc,gijcm->gijkm', table, piece, precision=highest)  104 us
    all_gather x1, local copies, waits for them, and re-layouts, per_device(): piece = lax.all_gather(section, 'gz', axis=3, tiled=True)  98 us
    dot_general x18, matrix products, correlate(): jnp.einsum('xpqm,pqyz->xyzm', padded[offset:offset + out_sizes[0]], table...  72.2 us
  transfers between devices with their start and end apart: 13, of which 10 were waited for; matrix products, arithmetic and copies ran while one was open for 6% of the time, Pallas kernels for 0%

commit v1 on v0

v1 whole, which is shorter than its diff:
```python
import jax
import jax.numpy as jnp
import numpy as np
import ml_dtypes
from jax import lax
from jax.experimental import pallas as pl
from jax.experimental.pallas import tpu as pltpu
from jax.sharding import PartitionSpec as P

M = 16
GAUSS = 8
MESH = pl.DeviceIdType.MESH
F32 = jnp.float32
BF16 = jnp.bfloat16


def weight(offset):
    return {0: 1.0, 1: 9 / 16, 3: -1 / 16}.get(abs(offset), 0.0)


def halo_list(side, size):
    if side == 0:
        return [size, size + 1, size + 2, size + 3, size + 5, None, None, None]
    return [-9, -7, -6, -5, -4, -3, -2, -1]


def extra_list(side, size):
    return [size + 1] if side == 0 else [-3, -1]


def cross(xs, ys):
    return [None if (x is None or y is None) else (x, y) for x in xs for y in ys]


def moved(coords, dx, dy):
    return [None if c is None else (c[0] + dx, c[1] + dy) for c in coords]


def padded(coords, size):
    return coords + [None] * (size - len(coords))


def picker(source, target):
    where = {c: i for i, c in enumerate(source) if c is not None}
    table = np.zeros((len(source), len(target)), np.float32)
    for j, c in enumerate(target):
        if c in where:
            table[where[c], j] = 1.0
    return table


def weights_between(fine, coarse):
    table = np.zeros((len(fine), len(coarse)), np.float32)
    for i, f in enumerate(fine):
        if f is None:
            continue
        for j, c in enumerate(coarse):
            if c is not None:
                table[i, j] = weight(f[0] - 2 * c[0]) * weight(f[1] - 2 * c[1])
    return table


ROWS_A = 512
ROWS_C = 2560


def plane(gx, gy):
    yl, xl = halo_list(gy, 24), halo_list(gx, 16)
    own = cross(range(16), range(24))
    fine = own + cross(range(16), yl) + cross(xl, list(range(24)) + yl)
    mid_own = cross(range(8), range(12))
    xs = list(range(8)) + extra_list(gx, 8)
    ys = list(range(12)) + extra_list(gy, 12)
    extra = [c for c in cross(xs, ys) if c not in set(mid_own)]
    mid = padded(mid_own, 128) + padded(extra, 128)
    return own, fine, mid_own, mid


def constants():
    whole = np.zeros((4, ROWS_C, 768), np.float32)
    spread = np.full((4, 32, 512), 1e30, np.float32)
    for gx in range(2):
        for gy in range(2):
            v = gx * 2 + gy
            own, fine, mid_own, mid = plane(gx, gy)
            out = whole[v]
            dy = 24 if gy == 0 else -24
            dx = 16 if gx == 0 else -16
            other_y = plane(gx, 1 - gy)[1]
            other_x = plane(1 - gx, gy)[1]
            out[0:384, 256:384] = picker(own, moved(other_y[384:512], 0, dy))
            out[0:512, 0:256] = picker(fine[:512], moved(other_x[512:768], dx, 0))
            xs = range(0, 7) if gx == 0 else range(-3, 4)
            ys = range(0, 9) if gy == 0 else range(-3, 6)
            window = padded(cross(xs, ys), 64)
            inside = cross(
                range(0, 10) if gx == 0 else range(-2, 8), range(0, 14) if gy == 0 else range(-2, 12)
            )
            up = weights_between(own, inside).astype(np.float64) @ weights_between(inside, window)
            up = np.concatenate([up, up], axis=1)
            high = up.astype(ml_dtypes.bfloat16).astype(np.float64)
            out[0:384, 384:512] = high
            out[0:384, 512:640] = up - high
            rz = np.zeros((256, 128), np.float32)
            for j in range(256):
                for i in range(128):
                    rz[j, i] = weight(j - 2 * i)
            out[0:256, 640:768] = rz
            out[512:1280, 0:256] = weights_between(fine, mid)
            top = padded(cross(range(4), range(6)), 32)
            out[512:768, 256:768] = np.tile(weights_between(mid, top), (1, 16))
            lanes = [c if c in set(inside) else None for c in cross(range(-2, 14), range(-2, 30))]
            out[768:1152, 256:768] = weights_between(own, lanes)
            out[1280:2048] = picker(fine, cross(range(-4, 20), range(-4, 28)))
            blocks = []
            for bx in (0, dx // 2):
                for by in (0, dy // 2):
                    blocks += padded(moved(mid_own, bx, by), 128)
            out[2048:2560] = picker(blocks, cross(range(-6, 18), range(-6, 26)))
            for i, c in enumerate(top):
                if c is None:
                    continue
                for wx in range(2):
                    for wy in range(2):
                        for xi in range(7):
                            for yi in range(9):
                                d = (4 * gx + c[0] - wx - xi) ** 2 + (6 * gy + c[1] - 3 * wy - yi) ** 2
                                lane = (wx * 2 + wy) * 128 + xi * 9 + yi
                                spread[v, i, lane] = d
                                spread[v, i, lane + 64] = d
    return whole.astype(ml_dtypes.bfloat16), spread


def dot(a, b):
    return lax.dot_general(a, b, (((1,), (0,)), ((), ())), preferred_element_type=F32)


def dot_t(a, b):
    return lax.dot_general(a, b, (((1,), (1,)), ((), ())), preferred_element_type=F32)


def split(a):
    high = a.astype(BF16)
    return high, (a - high.astype(F32)).astype(BF16)


def widen(a, count):
    near, far = 9.0 / 16.0, -1.0 / 16.0
    odd = near * (a[1 : count + 1] + a[2 : count + 2]) + far * (a[0:count] + a[3 : count + 3])
    return odd


def interleave(even, odd):
    both = jnp.concatenate([even[:, None], odd[:, None]], axis=1)
    return both.reshape((2 * even.shape[0],) + even.shape[1:])


def kernel(
    q_ref, kf_ref, km_ref, gw_ref, gg_ref, cst_hbm, spread_ref, out_ref,
    cst, fq, py, px, fpad, tfine, tmid, fm, mpad, gath, sfine, smid, amat, dmat, rmat, ezr, wlo, whi,
    cst_sem, s1, r1, s2, r2, sg, rg, s3, r3,
):
    gx, gy, gz = lax.axis_index("gx"), lax.axis_index("gy"), lax.axis_index("gz")
    nz = lax.axis_size("gz")
    ox, oy = 1 - gx, 1 - gy
    up, down = lax.rem(gz + 1, nz), lax.rem(gz + nz - 1, nz)
    variant = gx * 2 + gy

    barrier = pltpu.get_barrier_semaphore()
    for peer in ((ox, gy, gz), (gx, oy, gz), (ox, oy, gz), (gx, oy, up), (gx, oy, down)):
        pl.semaphore_signal(barrier, inc=1, device_id=peer, device_id_type=MESH)

    @pl.loop(1, nz)
    def _(d):
        pl.semaphore_signal(
            barrier, inc=1, device_id=(gx, gy, lax.rem(gz + d, nz)), device_id_type=MESH
        )

    first = pltpu.make_async_copy(
        cst_hbm.at[variant, pl.ds(0, ROWS_A)], cst.at[pl.ds(0, ROWS_A)], cst_sem.at[0]
    )
    rest = pltpu.make_async_copy(
        cst_hbm.at[variant, pl.ds(ROWS_A, ROWS_C - ROWS_A)],
        cst.at[pl.ds(ROWS_A, ROWS_C - ROWS_A)],
        cst_sem.at[1],
    )
    first.start()
    rest.start()

    turned = q_ref[...].astype(F32).reshape(384, 256).T.astype(BF16)
    fq[4:20, :, 0:384] = turned.reshape(16, 16, 384)
    first.wait()
    py[...] = dot(turned, cst[0:384, 256:384]).astype(BF16).reshape(16, 16, 128)

    def build(k_ref, table):
        lane = lax.broadcasted_iota(jnp.int32, (9, 512), 1)
        row = lax.broadcasted_iota(jnp.int32, (9, 512), 0)
        base = jnp.zeros((9, 512), F32)
        for a in range(9):
            place = (lane == row + 32 * a).astype(F32).astype(BF16)
            base = base + lax.dot_general(
                k_ref[a], place, (((0,), (0,)), ((), ())), preferred_element_type=F32
            )
        for c in range(9):
            strip = pltpu.roll(
                jnp.broadcast_to(base[c : c + 1], (8, 512)), 0, 1, stride=1, stride_axis=0
            )

            @pl.loop(0, 16)
            def _(i):
                low = pltpu.roll(strip, 16 * i, 1)
                high = pltpu.roll(strip, 16 * i + 8, 1)
                table[c, pl.ds(pl.multiple_of(16 * i, 16), 16), :] = jnp.concatenate(
                    [low, high], axis=0
                ).astype(BF16)

    build(kf_ref, tfine)

    pl.semaphore_wait(barrier, nz - 1 + 5)

    def send(src, dst, sems, recvs, i, peer):
        copy = pltpu.make_async_remote_copy(
            src_ref=src, dst_ref=dst, send_sem=sems.at[i], recv_sem=recvs.at[i],
            device_id=peer, device_id_type=MESH,
        )
        copy.start()
        return copy

    ways = [
        (py.at[12:16], fq.at[0:4, :, 384:512], (gx, oy, up)),
        (py.at[0:4], fq.at[20:24, :, 384:512], (gx, oy, down)),
        (fq.at[16:20, :, 0:384], fq.at[0:4, :, 0:384], (gx, gy, up)),
        (fq.at[4:8, :, 0:384], fq.at[20:24, :, 0:384], (gx, gy, down)),
        (py, fq.at[4:20, :, 384:512], (gx, oy, gz)),
    ]
    one = [send(src, dst, s1, r1, i, peer) for i, (src, dst, peer) in enumerate(ways)]

    build(km_ref, tmid)
    rest.wait()
    node = gz * 4 - 3 + lax.broadcasted_iota(jnp.int32, (16, 128), 0)
    gap = (node - lax.broadcasted_iota(jnp.int32, (16, 128), 1)).astype(F32)
    exists = (node >= 0) & (node < 4 * nz)
    half = lax.rem(lax.broadcasted_iota(jnp.int32, (32, 512), 1), 128) < 64
    parts = []
    for g in range(GAUSS):
        width = jnp.full((16, 128), gw_ref[g], F32)
        ratio = gap / width
        parts.append(jnp.where(exists, jnp.exp(-(ratio * ratio)) / jnp.sqrt(width), 0.0))
        width = jnp.full((32, 512), gw_ref[g], F32)
        both = jnp.exp(-(spread_ref[variant] / (width * width))) * (gg_ref[g] / width)
        for table, keep in ((wlo, half), (whi, jnp.logical_not(half))):
            high, low = split(jnp.where(keep, both, 0.0))
            table[0, 32 * g : 32 * g + 32] = high
            table[1, 32 * g : 32 * g + 32] = low
    ez = jnp.concatenate(parts, axis=0)
    rz = cst[0:256, 640:768]
    high, low = split(ez)
    low2 = (ez - high.astype(F32) - low.astype(F32)).astype(BF16)
    high, low = split(dot_t(high, rz) + dot_t(low, rz) + dot_t(low2, rz))
    ezr[0] = high
    ezr[1] = low

    for copy in one:
        copy.wait_recv()
    keep_low = (gz > 0).astype(F32).astype(BF16)
    keep_high = (gz < nz - 1).astype(F32).astype(BF16)
    fq[0:4, :, 0:512] = fq[0:4, :, 0:512] * keep_low
    fq[20:24, :, 0:512] = fq[20:24, :, 0:512] * keep_high
    known = fq[:, :, 0:512].reshape(384, 512)
    px[...] = dot(known, cst[0:512, 0:256]).astype(BF16).reshape(24, 16, 256)
    cross_x = send(px, fq.at[:, :, 512:768], s1, r1, 5, (ox, gy, gz))
    plane_mid = dot(known, cst[512:1024, 0:256])
    cross_x.wait_recv()
    plane_mid = plane_mid + dot(fq[:, :, 512:768].reshape(384, 256), cst[1024:1280, 0:256])
    rows = plane_mid.reshape(12, 2, 16, 256)
    even, odd = rows[:, 0], rows[:, 1]
    q_mid = (
        even[2:10]
        + (9.0 / 16.0) * (odd[1:9] + odd[2:10])
        + (-1.0 / 16.0) * (odd[0:8] + odd[3:11])
    ).astype(BF16)
    fm[6:14, :, 0:128] = q_mid[:, :, 0:128]
    tops = dot(q_mid.reshape(128, 256), cst[512:768, 256:768]).reshape(8, 16, 512)
    member = lax.broadcasted_iota(jnp.int32, (16, 512), 0)
    group = lax.broadcasted_iota(jnp.int32, (16, 512), 1) // 32
    gath[gz] = jnp.sum(jnp.where((member == group)[None], tops, 0.0), axis=1)

    def gather(d, slot):
        return pltpu.make_async_remote_copy(
            src_ref=gath.at[slot], dst_ref=gath.at[slot], send_sem=sg.at[d], recv_sem=rg.at[slot],
            device_id=(gx, gy, lax.rem(gz + d, nz)), device_id_type=MESH,
        )

    @pl.loop(1, nz)
    def _(d):
        gather(d, gz).start()

    ways = [
        (fm.at[8:14, :, 0:128], fm.at[0:6, :, 128:256], (gx, oy, up)),
        (fm.at[6:12, :, 0:128], fm.at[14:20, :, 128:256], (gx, oy, down)),
        (fm.at[8:14, :, 0:128], fm.at[0:6, :, 0:128], (gx, gy, up)),
        (fm.at[6:12, :, 0:128], fm.at[14:20, :, 0:128], (gx, gy, down)),
        (fm.at[6:14, :, 0:128], fm.at[6:14, :, 128:256], (gx, oy, gz)),
    ]
    two = [send(src, dst, s2, r2, i, peer) for i, (src, dst, peer) in enumerate(ways)]

    fpad[...] = dot(fq[...].reshape(384, 768), cst[1280:2048, :]).astype(BF16)
    sfine[...] = jnp.zeros_like(sfine)

    @pl.loop(0, 9)
    def _(c):
        rows_c = pl.ds(pl.multiple_of(c * 16, 16), 256)
        for g in range(2):
            sfine[g] += dot_t(tfine[c], fpad[rows_c, 256 * g : 256 * g + 512])

    for copy in two:
        copy.wait_recv()
    fm[0:6, :, 0:256] = fm[0:6, :, 0:256] * keep_low
    fm[14:20, :, 0:256] = fm[14:20, :, 0:256] * keep_high
    cross_m = send(fm.at[:, :, 0:256], fm.at[:, :, 256:512], s2, r2, 5, (ox, gy, gz))

    @pl.loop(1, nz)
    def _(d):
        gather(d, lax.rem(gz + nz - d, nz)).wait_recv()

    high, low = split(gath[...].reshape(256, 512))
    fields = dot(ezr[0], high) + (dot(ezr[0], low) + dot(ezr[1], high))
    lane = lax.broadcasted_iota(jnp.int32, (16, 128), 1) // 32
    for j in range(4):
        tile = fields[:, 128 * j : 128 * j + 128]
        turns = [tile] + [pltpu.roll(tile, 32 * t, 1) for t in range(1, 4)]
        for i in range(4):
            m = 4 * j + i
            for t in range(2):
                block = None
                for s in range(4):
                    g = 4 * t + s
                    piece = turns[(s - i) % 4][16 * g : 16 * g + 16]
                    block = piece if block is None else jnp.where(lane == s, piece, block)
                amat[16 * m : 16 * m + 16, 128 * t : 128 * t + 128] = block
    high, low = split(amat[...])
    share = dot(high[0:128], wlo[0]) + dot(high[128:256], whi[0])
    share = share + (dot(low[0:128], wlo[0]) + dot(low[128:256], whi[0]))
    share = share + (dot(high[0:128], wlo[1]) + dot(high[128:256], whi[1]))
    share = jnp.swapaxes(share.reshape(8, 16, 512), 0, 1)
    for w in range(4):
        dmat[w] = share[0:10, :, 128 * w : 128 * w + 128]
    ways = [(oy + 2 * gx, (gx, oy, gz)), (oy + 2 * ox, (ox, oy, gz)), (gy + 2 * ox, (ox, gy, gz))]
    three = [send(dmat.at[w], rmat.at[i], s3, r3, i, peer) for i, (w, peer) in enumerate(ways)]

    cross_m.wait_recv()
    mpad[...] = dot(fm[...].reshape(320, 512), cst[2048:2560, :]).astype(BF16)
    smid[...] = jnp.zeros_like(smid)

    @pl.loop(0, 9)
    def _(c):
        rows_c = pl.ds(pl.multiple_of(c * 16, 16), 192)
        for g in range(2):
            smid[:, 256 * g : 256 * g + 256] += dot_t(
                mpad[rows_c, 256 * g : 256 * g + 512], tmid[c]
            )

    def trimmed(mid):
        spot = lax.broadcasted_iota(jnp.int32, mid.shape, 0) - 2 + 8 * gz
        return jnp.where((spot >= 0) & (spot < 8 * nz), mid, 0.0)

    mid = trimmed(smid[...].reshape(12, 16, 512))
    fine = interleave(mid[2:10], widen(mid[1:12], 8)).reshape(256, 512)
    high, low = split(fine)
    back = cst[768:1152, 256:768]
    total = dot_t(back, high) + dot_t(back, low)
    total = total + sfine[...].reshape(16, 32, 256)[:, 0:24].reshape(384, 256)
    sfine_own = total

    for copy in three:
        copy.wait_recv()
    top = (dmat[variant] + rmat[2]) + (rmat[0] + rmat[1])
    mid = interleave(top[2:8], widen(top[1:10], 6))
    mid = trimmed(mid)
    fine = interleave(mid[2:10], widen(mid[1:12], 8))
    lower = lax.broadcasted_iota(jnp.int32, (16, 8, 128), 2) < 64
    fine = jnp.concatenate(
        [jnp.where(lower, fine, 0.0), jnp.where(lower, 0.0, fine)], axis=1
    ).reshape(256, 128)
    high, low = split(fine)
    up_high, up_low = cst[0:384, 384:512], cst[0:384, 512:640]
    result = dot_t(up_high, high) + (dot_t(up_high, low) + dot_t(up_low, high)) + sfine_own
    out_ref[...] = result.reshape(16, 24, 256)

    for copy in one + [cross_x] + two + [cross_m] + three:
        copy.wait_send()

    @pl.loop(1, nz)
    def _(d):
        gather(d, gz).wait_send()


def solution(mesh):
    whole, spread = constants()
    nz = mesh.shape["gz"]
    vmem = pl.BlockSpec(memory_space=pltpu.VMEM)
    smem = pl.BlockSpec(memory_space=pltpu.SMEM)
    dma = pltpu.SemaphoreType.DMA

    def per_device(charges, kernel_fine, kernel_mid, gauss_width, gauss_weight):
        return pl.pallas_call(
            kernel,
            out_shape=jax.ShapeDtypeStruct((16, 24, 256), F32),
            in_specs=[vmem, vmem, vmem, smem, smem, pl.BlockSpec(memory_space=pl.ANY), vmem],
            out_specs=vmem,
            scratch_shapes=[
                pltpu.VMEM((ROWS_C, 768), BF16),
                pltpu.VMEM((24, 16, 768), BF16),
                pltpu.VMEM((16, 16, 128), BF16),
                pltpu.VMEM((24, 16, 256), BF16),
                pltpu.VMEM((384, 768), BF16),
                pltpu.VMEM((9, 256, 512), BF16),
                pltpu.VMEM((9, 256, 512), BF16),
                pltpu.VMEM((20, 16, 512), BF16),
                pltpu.VMEM((320, 768), BF16),
                pltpu.VMEM((nz, 8, 512), F32),
                pltpu.VMEM((2, 256, 256), F32),
                pltpu.VMEM((192, 512), F32),
                pltpu.VMEM((256, 256), F32),
                pltpu.VMEM((4, 10, 8, 128), F32),
                pltpu.VMEM((3, 10, 8, 128), F32),
                pltpu.VMEM((2, 128, 256), BF16),
                pltpu.VMEM((2, 256, 512), BF16),
                pltpu.VMEM((2, 256, 512), BF16),
                dma((2,)),
                dma((6,)), dma((6,)),
                dma((6,)), dma((6,)),
                dma((nz,)), dma((nz,)),
                dma((3,)), dma((3,)),
            ],
            compiler_params=pltpu.CompilerParams(
                collective_id=0, has_side_effects=True, vmem_limit_bytes=48 * 2**20
            ),
        )(
            charges, kernel_fine, kernel_mid, gauss_width, gauss_weight,
            jnp.asarray(whole), jnp.asarray(spread),
        )

    placed = (P("gx", "gy", "gz"), P(), P(), P(), P())
    return jax.shard_map(
        per_device, mesh=mesh, in_specs=placed, out_specs=P("gx", "gy", "gz"), check_vma=False
    )
```

time: 2220 us -> 58.2 us (0.03)
  waiting for transfers between devices: 1680 us -> 0 us
  matrix products: 261 us -> 0 us
  local copies, waits for them, and re-layouts: 182 us -> 5.47 us
  Pallas kernels: 0 us -> 52.4 us
  blocking collectives: 41.6 us -> 0 us
  starting transfers between devices: 27 us -> 0 us
    all_gather x1 -> x0, waiting for transfers between devices: 1620 us -> none  [per_device(): piece = lax.all_gather(section, 'gz', axis=3, tiled=True)]
    dot_general x51 -> x0, matrix products: 261 us -> none  [the longest x1 104 us: per_device(): section = jnp.einsum('gkc,gijcm->gijkm', table, piece, precision=highest)]
    all_gather x1 -> x0, local copies, waits for them, and re-layouts: 98 us -> none  [per_device(): piece = lax.all_gather(section, 'gz', axis=3, tiled=True)]
    ppermute x12 -> x0, waiting for transfers between devices: 52.5 us -> none  [the longest x6 34.8 us: padded_2(): lax.ppermute(head, axis, [((i + 1) % count, i) for i in range(ends)])]
    pallas_call x0 -> x1, Pallas kernels: none -> 52.4 us  [per_device(): pl.pallas_call(kernel, out_shape=jax.ShapeDtypeStruct((16, 24, 256), F32)...]
    all_gather x2 -> x0, blocking collectives: 41.6 us -> none  [the longest x1 37.8 us: per_device(): piece = lax.all_gather(section, 'gy', axis=2, tiled=True)]
    convert_element_type x9 -> x0, local copies, waits for them, and re-layouts: 33.7 us -> none  [correlate(): table = jnp.einsum('bc,bpy,cqz->pqyz', kernel[offset], pick_y, pick_z, pr...]
    ppermute x12 -> x0, starting transfers between devices: 27 us -> none  [the longest x6 14.3 us: padded_2(): lax.ppermute(tail, axis, [(i, (i + 1) % count) for i in range(ends)])]
  transfers between devices with their start and end apart: 13 -> 0, of which waited for: 10 -> 0; matrix products, arithmetic and copies ran while one was open for 6% -> 0% of each run, Pallas kernels for 0% -> 0%
where the time goes in v1:
time: 58.2 us; the launch traced here: 57.9 us
  Pallas kernels  52.4 us (90%)
  local copies, waits for them, and re-layouts  5.47 us (9%)
    pallas_call x1, Pallas kernels, per_device(): pl.pallas_call(kernel, out_shape=jax.ShapeDtypeStruct((16, 24, 256), F32)...  52.4 us
    unnamed x13, local copies, waits for them, and re-layouts  5.47 us

profile of v1, /device:TPU:1, one launch (start us, length us, event | category | flops | bytes accessed | tf_op | source)
XLA Modules:
  0.0 57.9 jit_solution(7711052456817673794)
XLA Ops:
  0.0 0.0 copy-start
  0.0 0.9 %copy-done = f32[4,32,512]{2,1,0:T(8,128)S(1)} copy-done((f32[4,32,512]{2,1,0:T(8,128)S(1)}, f32[4,32,512]{2,1,0:T(8,128)}, u32[]{:S(2)}) %copy-start) | copy-done | bytes 262168
  1.0 0.0 copy-start.1
  1.0 0.9 %copy-done.1 = bf16[16,24,256]{2,1,0:T(8,128)(2,1)S(1)} copy-done((bf16[16,24,256]{2,1,0:T(8,128)(2,1)S(1)}, bf16[16,24,256]{2,1,0:T(8,128)(2,1)}, u32[]{:S(2)}) %copy-start.1) | copy-done | bytes 196632
  1.9 0.0 copy-start.2
  1.9 0.8 %copy-done.2 = bf16[9,9,9]{2,1,0:T(8,128)(2,1)S(1)} copy-done((bf16[9,9,9]{2,1,0:T(8,128)(2,1)S(1)}, bf16[9,9,9]{2,1,0:T(8,128)(2,1)}, u32[]{:S(2)}) %copy-start.2) | copy-done | bytes 1482
  2.6 0.0 copy-start.3
  2.6 0.8 %copy-done.3 = bf16[9,9,9]{2,1,0:T(8,128)(2,1)S(1)} copy-done((bf16[9,9,9]{2,1,0:T(8,128)(2,1)S(1)}, bf16[9,9,9]{2,1,0:T(8,128)(2,1)}, u32[]{:S(2)}) %copy-start.3) | copy-done | bytes 1482
  3.4 0.0 copy-start.4
  3.4 0.7 %copy-done.4 = f32[8]{0:T(128)S(1)} copy-done((f32[8]{0:T(128)S(1)}, f32[8]{0:T(128)}, u32[]{:S(2)}) %copy-start.4) | copy-done | bytes 56
  4.1 0.0 copy-start.5
  4.1 0.7 %copy-done.5 = f32[8]{0:T(128)S(1)} copy-done((f32[8]{0:T(128)S(1)}, f32[8]{0:T(128)}, u32[]{:S(2)}) %copy-start.5) | copy-done | bytes 56
  4.7 52.4 %shard_map.73 = f32[16,24,256]{2,1,0:T(8,128)S(1)} custom-call(bf16[16,24,256]{2,1,0:T(8,128)(2,1)S(1)} %copy-done.1, bf16[9,9,9]{2,1,0:T(8,128)(2,1)S(1)} %copy-done.2, bf16[9,9,9]{2,1,0:T(8,128)(2,1)S(1)} %copy-done.3, f32[8]{0:T(128)S(1)} %copy-done.4, f32[8]{0:T(128)S(1)} %copy-done.5, bf16[4,2560,768]{2,1,0:T(8,128)(2,1)} %constant.4.clone.cst_hbm, ...), custom_call_target="tpu_custom_call" | custom-call | tf_op jit(solution)/shard_map/pallas_call | solution.py:406
  57.1 0.7 %copy.9 = f32[16,24,256]{2,1,0:T(8,128)} copy(f32[16,24,256]{2,1,0:T(8,128)S(1)} %shard_map.73) | data formatting | bytes 786432
Async XLA Ops:
  0.0 0.9 %copy-start = (f32[4,32,512]{2,1,0:T(8,128)S(1)}, f32[4,32,512]{2,1,0:T(8,128)}, u32[]{:S(2)}) copy-start(f32[4,32,512]{2,1,0:T(8,128)} %constant.5.clone.spread_ref) | copy-start | bytes 786436
  1.0 0.9 %copy-start.1 = (bf16[16,24,256]{2,1,0:T(8,128)(2,1)S(1)}, bf16[16,24,256]{2,1,0:T(8,128)(2,1)}, u32[]{:S(2)}) copy-start(bf16[16,24,256]{2,1,0:T(8,128)(2,1)} %q_ref.1) | copy-start | bytes 589828
  1.9 0.8 %copy-start.2 = (bf16[9,9,9]{2,1,0:T(8,128)(2,1)S(1)}, bf16[9,9,9]{2,1,0:T(8,128)(2,1)}, u32[]{:S(2)}) copy-start(bf16[9,9,9]{2,1,0:T(8,128)(2,1)} %kf_ref.1) | copy-start | bytes 4378
  2.6 0.8 %copy-start.3 = (bf16[9,9,9]{2,1,0:T(8,128)(2,1)S(1)}, bf16[9,9,9]{2,1,0:T(8,128)(2,1)}, u32[]{:S(2)}) copy-start(bf16[9,9,9]{2,1,0:T(8,128)(2,1)} %km_ref.1) | copy-start | bytes 4378
  3.4 0.7 %copy-start.4 = (f32[8]{0:T(128)S(1)}, f32[8]{0:T(128)}, u32[]{:S(2)}) copy-start(f32[8]{0:T(128)} %gw_ref.1) | copy-start | bytes 100
  4.1 0.7 %copy-start.5 = (f32[8]{0:T(128)S(1)}, f32[8]{0:T(128)}, u32[]{:S(2)}) copy-start(f32[8]{0:T(128)} %gg_ref.1) | copy-start | bytes 100

commit v2 on v1

--- a/solution.py
+++ b/solution.py
@@ -156,8 +156,8 @@
 
 
 def kernel(
-    q_ref, kf_ref, km_ref, gw_ref, gg_ref, cst_hbm, spread_ref, out_ref,
-    cst, fq, py, px, fpad, tfine, tmid, fm, mpad, gath, sfine, smid, amat, dmat, rmat, ezr, wlo, whi,
+    q_hbm, kf_hbm, km_hbm, gw_hbm, gg_hbm, cst_hbm, spread_hbm, out_ref,
+    q_ref, kf_ref, km_ref, gw_ref, gg_ref, spread_ref, base, cst, fq, py, px, fpad, tfine, tmid, fm, mpad, gath, sfine, smid, amat, dmat, rmat, ezr, wlo, whi,
     cst_sem, s1, r1, s2, r2, sg, rg, s3, r3,
 ):
     gx, gy, gz = lax.axis_index("gx"), lax.axis_index("gy"), lax.axis_index("gz")
@@ -165,16 +165,6 @@
     ox, oy = 1 - gx, 1 - gy
     up, down = lax.rem(gz + 1, nz), lax.rem(gz + nz - 1, nz)
     variant = gx * 2 + gy
-
-    barrier = pltpu.get_barrier_semaphore()
-    for peer in ((ox, gy, gz), (gx, oy, gz), (ox, oy, gz), (gx, oy, up), (gx, oy, down)):
-        pl.semaphore_signal(barrier, inc=1, device_id=peer, device_id_type=MESH)
-
-    @pl.loop(1, nz)
-    def _(d):
-        pl.semaphore_signal(
-            barrier, inc=1, device_id=(gx, gy, lax.rem(gz + d, nz)), device_id_type=MESH
-        )
 
     first = pltpu.make_async_copy(
         cst_hbm.at[variant, pl.ds(0, ROWS_A)], cst.at[pl.ds(0, ROWS_A)], cst_sem.at[0]
@@ -184,9 +174,33 @@
         cst.at[pl.ds(ROWS_A, ROWS_C - ROWS_A)],
         cst_sem.at[1],
     )
+    inputs = [
+        pltpu.make_async_copy(src, dst, cst_sem.at[2 + i])
+        for i, (src, dst) in enumerate(
+            (
+                (q_hbm, q_ref), (kf_hbm, kf_ref), (km_hbm, km_ref), (gw_hbm, gw_ref),
+                (gg_hbm, gg_ref), (spread_hbm.at[variant], spread_ref),
+            )
+        )
+    ]
+    for copy in inputs[:2]:
+        copy.start()
     first.start()
+    for copy in inputs[2:]:
+        copy.start()
     rest.start()
 
+    barrier = pltpu.get_barrier_semaphore()
+    for peer in ((ox, gy, gz), (gx, oy, gz), (ox, oy, gz), (gx, oy, up), (gx, oy, down)):
+        pl.semaphore_signal(barrier, inc=1, device_id=peer, device_id_type=MESH)
+
+    @pl.loop(1, nz)
+    def _(d):
+        pl.semaphore_signal(
+            barrier, inc=1, device_id=(gx, gy, lax.rem(gz + d, nz)), device_id_type=MESH
+        )
+
+    inputs[0].wait()
     turned = q_ref[...].astype(F32).reshape(384, 256).T.astype(BF16)
     fq[4:20, :, 0:384] = turned.reshape(16, 16, 384)
     first.wait()
@@ -195,25 +209,25 @@
     def build(k_ref, table):
         lane = lax.broadcasted_iota(jnp.int32, (9, 512), 1)
         row = lax.broadcasted_iota(jnp.int32, (9, 512), 0)
-        base = jnp.zeros((9, 512), F32)
+        total = jnp.zeros((9, 512), F32)
         for a in range(9):
             place = (lane == row + 32 * a).astype(F32).astype(BF16)
-            base = base + lax.dot_general(
+            total = total + lax.dot_general(
                 k_ref[a], place, (((0,), (0,)), ((), ())), preferred_element_type=F32
             )
-        for c in range(9):
-            strip = pltpu.roll(
-                jnp.broadcast_to(base[c : c + 1], (8, 512)), 0, 1, stride=1, stride_axis=0
-            )
-
-            @pl.loop(0, 16)
-            def _(i):
-                low = pltpu.roll(strip, 16 * i, 1)
-                high = pltpu.roll(strip, 16 * i + 8, 1)
-                table[c, pl.ds(pl.multiple_of(16 * i, 16), 16), :] = jnp.concatenate(
-                    [low, high], axis=0
-                ).astype(BF16)
-
+        base[0:9] = total
+
+        @pl.loop(0, 9)
+        def _(c):
+            line = jnp.broadcast_to(base[pl.ds(c, 1)], (16, 512))
+            strip = pltpu.roll(line, 0, 1, stride=1, stride_axis=0)
+            for i in range(8):
+                part = pltpu.roll(strip, 16 * i, 1).astype(BF16)
+                table[c, 16 * i : 16 * i + 16, :] = part
+                table[c, 128 + 16 * i : 144 + 16 * i, 0:128] = part[:, 384:512]
+                table[c, 128 + 16 * i : 144 + 16 * i, 128:512] = part[:, 0:384]
+
+    inputs[1].wait()
     build(kf_ref, tfine)
 
     pl.semaphore_wait(barrier, nz - 1 + 5)
@@ -235,6 +249,8 @@
     ]
     one = [send(src, dst, s1, r1, i, peer) for i, (src, dst, peer) in enumerate(ways)]
 
+    for copy in inputs[2:]:
+        copy.wait()
     build(km_ref, tmid)
     rest.wait()
     node = gz * 4 - 3 + lax.broadcasted_iota(jnp.int32, (16, 128), 0)
@@ -247,7 +263,7 @@
         ratio = gap / width
         parts.append(jnp.where(exists, jnp.exp(-(ratio * ratio)) / jnp.sqrt(width), 0.0))
         width = jnp.full((32, 512), gw_ref[g], F32)
-        both = jnp.exp(-(spread_ref[variant] / (width * width))) * (gg_ref[g] / width)
+        both = jnp.exp(-(spread_ref[...] / (width * width))) * (gg_ref[g] / width)
         for table, keep in ((wlo, half), (whi, jnp.logical_not(half))):
             high, low = split(jnp.where(keep, both, 0.0))
             table[0, 32 * g : 32 * g + 32] = high
@@ -305,13 +321,12 @@
     two = [send(src, dst, s2, r2, i, peer) for i, (src, dst, peer) in enumerate(ways)]
 
     fpad[...] = dot(fq[...].reshape(384, 768), cst[1280:2048, :]).astype(BF16)
-    sfine[...] = jnp.zeros_like(sfine)
-
-    @pl.loop(0, 9)
-    def _(c):
-        rows_c = pl.ds(pl.multiple_of(c * 16, 16), 256)
-        for g in range(2):
-            sfine[g] += dot_t(tfine[c], fpad[rows_c, 256 * g : 256 * g + 512])
+    for g in range(2):
+        total = None
+        for c in range(9):
+            term = dot_t(tfine[c], fpad[16 * c : 16 * c + 256, 256 * g : 256 * g + 512])
+            total = term if total is None else total + term
+        sfine[g] = total
 
     for copy in two:
         copy.wait_recv()
@@ -350,15 +365,12 @@
 
     cross_m.wait_recv()
     mpad[...] = dot(fm[...].reshape(320, 512), cst[2048:2560, :]).astype(BF16)
-    smid[...] = jnp.zeros_like(smid)
-
-    @pl.loop(0, 9)
-    def _(c):
-        rows_c = pl.ds(pl.multiple_of(c * 16, 16), 192)
-        for g in range(2):
-            smid[:, 256 * g : 256 * g + 256] += dot_t(
-                mpad[rows_c, 256 * g : 256 * g + 512], tmid[c]
-            )
+    for g in range(2):
+        total = None
+        for c in range(9):
+            term = dot_t(mpad[16 * c : 16 * c + 192, 256 * g : 256 * g + 512], tmid[c])
+            total = term if total is None else total + term
+        smid[:, 256 * g : 256 * g + 256] = total
 
     def trimmed(mid):
         spot = lax.broadcasted_iota(jnp.int32, mid.shape, 0) - 2 + 8 * gz
@@ -399,16 +411,22 @@
     whole, spread = constants()
     nz = mesh.shape["gz"]
     vmem = pl.BlockSpec(memory_space=pltpu.VMEM)
-    smem = pl.BlockSpec(memory_space=pltpu.SMEM)
     dma = pltpu.SemaphoreType.DMA
 
     def per_device(charges, kernel_fine, kernel_mid, gauss_width, gauss_weight):
         return pl.pallas_call(
             kernel,
             out_shape=jax.ShapeDtypeStruct((16, 24, 256), F32),
-            in_specs=[vmem, vmem, vmem, smem, smem, pl.BlockSpec(memory_space=pl.ANY), vmem],
+            in_specs=[pl.BlockSpec(memory_space=pltpu.HBM)] * 7,
             out_specs=vmem,
             scratch_shapes=[
+                pltpu.VMEM((16, 24, 256), BF16),
+                pltpu.VMEM((9, 9, 9), BF16),
+                pltpu.VMEM((9, 9, 9), BF16),
+                pltpu.SMEM((GAUSS,), F32),
+                pltpu.SMEM((GAUSS,), F32),
+                pltpu.VMEM((32, 512), F32),
+                pltpu.VMEM((16, 512), F32),
                 pltpu.VMEM((ROWS_C, 768), BF16),
                 pltpu.VMEM((24, 16, 768), BF16),
                 pltpu.VMEM((16, 16, 128), BF16),
@@ -427,7 +445,7 @@
                 pltpu.VMEM((2, 128, 256), BF16),
                 pltpu.VMEM((2, 256, 512), BF16),
                 pltpu.VMEM((2, 256, 512), BF16),
-                dma((2,)),
+                dma((8,)),
                 dma((6,)), dma((6,)),
                 dma((6,)), dma((6,)),
                 dma((nz,)), dma((nz,)),

time: 58.2 us -> 41 us (0.70)
  Pallas kernels: 52.4 us -> 35.2 us
    pallas_call x1, Pallas kernels: 52.4 us -> 35.2 us  [per_device(): pl.pallas_call(kernel, out_shape=jax.ShapeDtypeStruct((16, 24, 256), F32)...]
where the time goes in v2:
time: 41 us; the launch traced here: 40.7 us
  Pallas kernels  35.2 us (86%)
  local copies, waits for them, and re-layouts  5.47 us (13%)
    pallas_call x1, Pallas kernels, per_device(): pl.pallas_call(kernel, out_shape=jax.ShapeDtypeStruct((16, 24, 256), F32)...  35.2 us
    unnamed x13, local copies, waits for them, and re-layouts  5.47 us

profile of v2, /device:TPU:1, one launch (start us, length us, event | category | flops | bytes accessed | tf_op | source)
XLA Modules:
  0.0 40.7 jit_solution(13451115520059190740)
XLA Ops:
  0.0 0.0 copy-start
  0.0 0.9 %copy-done = f32[4,32,512]{2,1,0:T(8,128)S(1)} copy-done((f32[4,32,512]{2,1,0:T(8,128)S(1)}, f32[4,32,512]{2,1,0:T(8,128)}, u32[]{:S(2)}) %copy-start) | copy-done | bytes 262168
  1.0 0.0 copy-start.1
  1.0 0.9 %copy-done.1 = bf16[16,24,256]{2,1,0:T(8,128)(2,1)S(1)} copy-done((bf16[16,24,256]{2,1,0:T(8,128)(2,1)S(1)}, bf16[16,24,256]{2,1,0:T(8,128)(2,1)}, u32[]{:S(2)}) %copy-start.1) | copy-done | bytes 196632
  1.9 0.0 copy-start.2
  1.9 0.8 %copy-done.2 = bf16[9,9,9]{2,1,0:T(8,128)(2,1)S(1)} copy-done((bf16[9,9,9]{2,1,0:T(8,128)(2,1)S(1)}, bf16[9,9,9]{2,1,0:T(8,128)(2,1)}, u32[]{:S(2)}) %copy-start.2) | copy-done | bytes 1482
  2.6 0.0 copy-start.3
  2.6 0.8 %copy-done.3 = bf16[9,9,9]{2,1,0:T(8,128)(2,1)S(1)} copy-done((bf16[9,9,9]{2,1,0:T(8,128)(2,1)S(1)}, bf16[9,9,9]{2,1,0:T(8,128)(2,1)}, u32[]{:S(2)}) %copy-start.3) | copy-done | bytes 1482
  3.4 0.0 copy-start.4
  3.4 0.7 %copy-done.4 = f32[8]{0:T(128)S(1)} copy-done((f32[8]{0:T(128)S(1)}, f32[8]{0:T(128)}, u32[]{:S(2)}) %copy-start.4) | copy-done | bytes 56
  4.1 0.0 copy-start.5
  4.1 0.7 %copy-done.5 = f32[8]{0:T(128)S(1)} copy-done((f32[8]{0:T(128)S(1)}, f32[8]{0:T(128)}, u32[]{:S(2)}) %copy-start.5) | copy-done | bytes 56
  4.7 35.2 %shard_map.73 = f32[16,24,256]{2,1,0:T(8,128)S(1)} custom-call(bf16[16,24,256]{2,1,0:T(8,128)(2,1)S(1)} %copy-done.1, bf16[9,9,9]{2,1,0:T(8,128)(2,1)S(1)} %copy-done.2, bf16[9,9,9]{2,1,0:T(8,128)(2,1)S(1)} %copy-done.3, f32[8]{0:T(128)S(1)} %copy-done.4, f32[8]{0:T(128)S(1)} %copy-done.5, bf16[4,2560,768]{2,1,0:T(8,128)(2,1)} %constant.4.clone.cst_hbm, ...), custom_call_target="tpu_custom_call" | custom-call | tf_op jit(solution)/shard_map/pallas_call | solution.py:417
  39.9 0.7 %copy.9 = f32[16,24,256]{2,1,0:T(8,128)} copy(f32[16,24,256]{2,1,0:T(8,128)S(1)} %shard_map.73) | data formatting | bytes 786432
Async XLA Ops:
  0.0 0.9 %copy-start = (f32[4,32,512]{2,1,0:T(8,128)S(1)}, f32[4,32,512]{2,1,0:T(8,128)}, u32[]{:S(2)}) copy-start(f32[4,32,512]{2,1,0:T(8,128)} %constant.5.clone.spread_hbm) | copy-start | bytes 786436
  1.0 0.9 %copy-start.1 = (bf16[16,24,256]{2,1,0:T(8,128)(2,1)S(1)}, bf16[16,24,256]{2,1,0:T(8,128)(2,1)}, u32[]{:S(2)}) copy-start(bf16[16,24,256]{2,1,0:T(8,128)(2,1)} %q_hbm.1) | copy-start | bytes 589828
  1.9 0.8 %copy-start.2 = (bf16[9,9,9]{2,1,0:T(8,128)(2,1)S(1)}, bf16[9,9,9]{2,1,0:T(8,128)(2,1)}, u32[]{:S(2)}) copy-start(bf16[9,9,9]{2,1,0:T(8,128)(2,1)} %kf_hbm.1) | copy-start | bytes 4378
  2.6 0.8 %copy-start.3 = (bf16[9,9,9]{2,1,0:T(8,128)(2,1)S(1)}, bf16[9,9,9]{2,1,0:T(8,128)(2,1)}, u32[]{:S(2)}) copy-start(bf16[9,9,9]{2,1,0:T(8,128)(2,1)} %km_hbm.1) | copy-start | bytes 4378
  3.4 0.7 %copy-start.4 = (f32[8]{0:T(128)S(1)}, f32[8]{0:T(128)}, u32[]{:S(2)}) copy-start(f32[8]{0:T(128)} %gw_hbm.1) | copy-start | bytes 100
  4.1 0.7 %copy-start.5 = (f32[8]{0:T(128)S(1)}, f32[8]{0:T(128)}, u32[]{:S(2)}) copy-start(f32[8]{0:T(128)} %gg_hbm.1) | copy-start | bytes 100

commit v3 on v2

--- a/solution.py
+++ b/solution.py
@@ -452,7 +452,7 @@
                 dma((3,)), dma((3,)),
             ],
             compiler_params=pltpu.CompilerParams(
-                collective_id=0, has_side_effects=True, vmem_limit_bytes=48 * 2**20
+                collective_id=0, has_side_effects=True, vmem_limit_bytes=63 * 2**20
             ),
         )(
             charges, kernel_fine, kernel_mid, gauss_width, gauss_weight,

time: 41 us -> 37.5 us (0.915)
  local copies, waits for them, and re-layouts: 5.47 us -> 1.77 us
    unnamed x13 -> x1, local copies, waits for them, and re-layouts: 5.47 us -> 1.77 us
where the time goes in v3:
time: 37.5 us; the launch traced here: 37.3 us
  Pallas kernels  35.6 us (95%)
  local copies, waits for them, and re-layouts  1.77 us (5%)
    pallas_call x1, Pallas kernels, per_device(): pl.pallas_call(kernel, out_shape=jax.ShapeDtypeStruct((16, 24, 256), F32)...  35.6 us
    unnamed x1, local copies, waits for them, and re-layouts  1.77 us

profile of v3, /device:TPU:1, one launch (start us, length us, event | category | flops | bytes accessed | tf_op | source)
XLA Modules:
  0.0 37.3 jit_solution(2737942008100408973)
XLA Ops:
  0.0 35.6 %shard_map.73 = f32[16,24,256]{2,1,0:T(8,128)} custom-call(bf16[16,24,256]{2,1,0:T(8,128)(2,1)} %q_hbm.1, bf16[9,9,9]{2,1,0:T(8,128)(2,1)} %kf_hbm.1, bf16[9,9,9]{2,1,0:T(8,128)(2,1)} %km_hbm.1, f32[8]{0:T(128)} %gw_hbm.1, f32[8]{0:T(128)} %gg_hbm.1, bf16[4,2560,768]{2,1,0:T(8,128)(2,1)} %constant.4.clone.cst_hbm, f32[4,32,512]{2,1,0:T(8,128)} %constant.5.clone.spread_hbm), custom_call_target="tpu_custom_call" | custom-call | tf_op jit(solution)/shard_map/pallas_call | solution.py:417
  35.6 1.8 %copy.9 = f32[16,24,256]{2,1,0:T(8,128)} copy(f32[16,24,256]{2,1,0:T(8,128)} %shard_map.73) | data formatting | bytes 786432

commit v4 on v3

--- a/solution.py
+++ b/solution.py
@@ -41,11 +41,11 @@
 
 
 def picker(source, target):
-    where = {c: i for i, c in enumerate(source) if c is not None}
     table = np.zeros((len(source), len(target)), np.float32)
     for j, c in enumerate(target):
-        if c in where:
-            table[where[c], j] = 1.0
+        for i, other in enumerate(source):
+            if c is not None and c == other:
+                table[i, j] = 1.0
     return table
 
 
@@ -65,14 +65,13 @@
 
 
 def plane(gx, gy):
-    yl, xl = halo_list(gy, 24), halo_list(gx, 16)
+    yl = [24, 25, 26, 27] if gy == 0 else [-4, -3, -2, -1]
+    xl = halo_list(gx, 16)
     own = cross(range(16), range(24))
-    fine = own + cross(range(16), yl) + cross(xl, list(range(24)) + yl)
+    edge = cross(range(16), yl)
+    fine = own + edge + edge + cross(xl, list(range(24)) + yl + [None] * 4)
     mid_own = cross(range(8), range(12))
-    xs = list(range(8)) + extra_list(gx, 8)
-    ys = list(range(12)) + extra_list(gy, 12)
-    extra = [c for c in cross(xs, ys) if c not in set(mid_own)]
-    mid = padded(mid_own, 128) + padded(extra, 128)
+    mid = padded(mid_own + cross(extra_list(gx, 8), range(12)), 128)
     return own, fine, mid_own, mid
 
 
@@ -105,10 +104,13 @@
             for j in range(256):
                 for i in range(128):
                     rz[j, i] = weight(j - 2 * i)
-            out[0:256, 640:768] = rz
-            out[512:1280, 0:256] = weights_between(fine, mid)
-            top = padded(cross(range(4), range(6)), 32)
-            out[512:768, 256:768] = np.tile(weights_between(mid, top), (1, 16))
+            empty = np.zeros((32, 8, 128), np.float32)
+            rz = rz.reshape(32, 8, 128)
+            out[0:512, 640:768] = np.stack([rz, empty], axis=1).reshape(512, 128)
+            out[512:1024, 128:256] = np.stack([empty, rz], axis=1).reshape(512, 128)
+            out[512:1280, 0:128] = weights_between(fine, mid)
+            top = cross(range(4), list(range(8)) if gy == 0 else list(range(-1, 6)) + [None])
+            out[512:640, 256:768] = np.tile(weights_between(mid, top), (1, 16))
             lanes = [c if c in set(inside) else None for c in cross(range(-2, 14), range(-2, 30))]
             out[768:1152, 256:768] = weights_between(own, lanes)
             out[1280:2048] = picker(fine, cross(range(-4, 20), range(-4, 28)))
@@ -157,7 +159,7 @@
 
 def kernel(
     q_hbm, kf_hbm, km_hbm, gw_hbm, gg_hbm, cst_hbm, spread_hbm, out_ref,
-    q_ref, kf_ref, km_ref, gw_ref, gg_ref, spread_ref, base, cst, fq, py, px, fpad, tfine, tmid, fm, mpad, gath, sfine, smid, amat, dmat, rmat, ezr, wlo, whi,
+    q_ref, kf_ref, km_ref, gw_ref, gg_ref, spread_ref, base, cst, fq, py, yb, yz, px, fpad, tfine, tmid, fm, mpad, gath, sfine, smid, amat, dmat, rmat, ezr, wlo, whi,
     cst_sem, s1, r1, s2, r2, sg, rg, s3, r3,
 ):
     gx, gy, gz = lax.axis_index("gx"), lax.axis_index("gy"), lax.axis_index("gz")
@@ -204,7 +206,9 @@
     turned = q_ref[...].astype(F32).reshape(384, 256).T.astype(BF16)
     fq[4:20, :, 0:384] = turned.reshape(16, 16, 384)
     first.wait()
-    py[...] = dot(turned, cst[0:384, 256:384]).astype(BF16).reshape(16, 16, 128)
+    edge = dot(turned, cst[0:384, 256:384]).reshape(16, 16, 128)
+    low_half = lax.broadcasted_iota(jnp.int32, (8, 16, 128), 2) < 64
+    py[...] = jnp.where(low_half, edge[0:8], edge[8:16]).astype(BF16)
 
     def build(k_ref, table):
         lane = lax.broadcasted_iota(jnp.int32, (9, 512), 1)
@@ -227,9 +231,6 @@
                 table[c, 128 + 16 * i : 144 + 16 * i, 0:128] = part[:, 384:512]
                 table[c, 128 + 16 * i : 144 + 16 * i, 128:512] = part[:, 0:384]
 
-    inputs[1].wait()
-    build(kf_ref, tfine)
-
     pl.semaphore_wait(barrier, nz - 1 + 5)
 
     def send(src, dst, sems, recvs, i, peer):
@@ -241,16 +242,17 @@
         return copy
 
     ways = [
-        (py.at[12:16], fq.at[0:4, :, 384:512], (gx, oy, up)),
-        (py.at[0:4], fq.at[20:24, :, 384:512], (gx, oy, down)),
+        (py.at[4:8], yz.at[0:4], (gx, oy, up)),
+        (py.at[0:4], yz.at[4:8], (gx, oy, down)),
         (fq.at[16:20, :, 0:384], fq.at[0:4, :, 0:384], (gx, gy, up)),
         (fq.at[4:8, :, 0:384], fq.at[20:24, :, 0:384], (gx, gy, down)),
-        (py, fq.at[4:20, :, 384:512], (gx, oy, gz)),
+        (py, yb, (gx, oy, gz)),
     ]
     one = [send(src, dst, s1, r1, i, peer) for i, (src, dst, peer) in enumerate(ways)]
 
-    for copy in inputs[2:]:
+    for copy in inputs[1:]:
         copy.wait()
+    build(kf_ref, tfine)
     build(km_ref, tmid)
     rest.wait()
     node = gz * 4 - 3 + lax.broadcasted_iota(jnp.int32, (16, 128), 0)
@@ -269,37 +271,50 @@
             table[0, 32 * g : 32 * g + 32] = high
             table[1, 32 * g : 32 * g + 32] = low
     ez = jnp.concatenate(parts, axis=0)
-    rz = cst[0:256, 640:768]
     high, low = split(ez)
     low2 = (ez - high.astype(F32) - low.astype(F32)).astype(BF16)
-    high, low = split(dot_t(high, rz) + dot_t(low, rz) + dot_t(low2, rz))
-    ezr[0] = high
-    ezr[1] = low
+    for h, rz in enumerate((cst[0:512, 640:768], cst[512:1024, 128:256])):
+        first_half, second = split(dot_t(high, rz) + dot_t(low, rz) + dot_t(low2, rz))
+        ezr[h, 0] = first_half
+        ezr[h, 1] = second
 
     for copy in one:
         copy.wait_recv()
     keep_low = (gz > 0).astype(F32).astype(BF16)
     keep_high = (gz < nz - 1).astype(F32).astype(BF16)
-    fq[0:4, :, 0:512] = fq[0:4, :, 0:512] * keep_low
-    fq[20:24, :, 0:512] = fq[20:24, :, 0:512] * keep_high
+    fq[0:4, :, 0:384] = fq[0:4, :, 0:384] * keep_low
+    fq[20:24, :, 0:384] = fq[20:24, :, 0:384] * keep_high
+    in_low = low_half.astype(F32).astype(BF16)
+    in_high = jnp.logical_not(low_half).astype(F32).astype(BF16)
+    fq[0:4, :, 384:512] = yz[0:4] * in_high[0:4] * keep_low
+    fq[4:12, :, 384:512] = yb[...] * in_low
+    fq[12:20, :, 384:512] = yb[...] * in_high
+    fq[20:24, :, 384:512] = yz[4:8] * in_low[0:4] * keep_high
     known = fq[:, :, 0:512].reshape(384, 512)
     px[...] = dot(known, cst[0:512, 0:256]).astype(BF16).reshape(24, 16, 256)
     cross_x = send(px, fq.at[:, :, 512:768], s1, r1, 5, (ox, gy, gz))
-    plane_mid = dot(known, cst[512:1024, 0:256])
+    plane_mid = dot(known, cst[512:1024, 0:128])
     cross_x.wait_recv()
-    plane_mid = plane_mid + dot(fq[:, :, 512:768].reshape(384, 256), cst[1024:1280, 0:256])
-    rows = plane_mid.reshape(12, 2, 16, 256)
+    plane_mid = plane_mid + dot(fq[:, :, 512:768].reshape(384, 256), cst[1024:1280, 0:128])
+    rows = plane_mid.reshape(12, 2, 16, 128)
     even, odd = rows[:, 0], rows[:, 1]
     q_mid = (
         even[2:10]
         + (9.0 / 16.0) * (odd[1:9] + odd[2:10])
         + (-1.0 / 16.0) * (odd[0:8] + odd[3:11])
     ).astype(BF16)
-    fm[6:14, :, 0:128] = q_mid[:, :, 0:128]
-    tops = dot(q_mid.reshape(128, 256), cst[512:768, 256:768]).reshape(8, 16, 512)
+    fm[6:14, :, 0:128] = q_mid
+    tops = dot(q_mid.reshape(128, 128), cst[512:640, 256:768]).reshape(8, 16, 512)
     member = lax.broadcasted_iota(jnp.int32, (16, 512), 0)
     group = lax.broadcasted_iota(jnp.int32, (16, 512), 1) // 32
-    gath[gz] = jnp.sum(jnp.where((member == group)[None], tops, 0.0), axis=1)
+    tops = jnp.sum(jnp.where((member == group)[None], tops, 0.0), axis=1)
+    sent, error = [], jnp.zeros((1, 512), F32)
+    for z in range(8):
+        value = tops[z : z + 1] + error
+        sent.append(value.astype(BF16).astype(F32))
+        error = value - sent[-1]
+    sent = jnp.concatenate(sent, axis=0)
+    gath[gz] = jnp.concatenate([sent[:, 0:256], sent[:, 256:512]], axis=0).astype(BF16)
 
     def gather(d, slot):
         return pltpu.make_async_remote_copy(
@@ -338,8 +353,8 @@
     def _(d):
         gather(d, lax.rem(gz + nz - d, nz)).wait_recv()
 
-    high, low = split(gath[...].reshape(256, 512))
-    fields = dot(ezr[0], high) + (dot(ezr[0], low) + dot(ezr[1], high))
+    got = gath[...].reshape(512, 256)
+    fields = jnp.concatenate([dot(ezr[h, 0], got) + dot(ezr[h, 1], got) for h in range(2)], axis=1)
     lane = lax.broadcasted_iota(jnp.int32, (16, 128), 1) // 32
     for j in range(4):
         tile = fields[:, 128 * j : 128 * j + 128]
@@ -429,20 +444,22 @@
                 pltpu.VMEM((16, 512), F32),
                 pltpu.VMEM((ROWS_C, 768), BF16),
                 pltpu.VMEM((24, 16, 768), BF16),
-                pltpu.VMEM((16, 16, 128), BF16),
+                pltpu.VMEM((8, 16, 128), BF16),
+                pltpu.VMEM((8, 16, 128), BF16),
+                pltpu.VMEM((8, 16, 128), BF16),
                 pltpu.VMEM((24, 16, 256), BF16),
                 pltpu.VMEM((384, 768), BF16),
                 pltpu.VMEM((9, 256, 512), BF16),
                 pltpu.VMEM((9, 256, 512), BF16),
                 pltpu.VMEM((20, 16, 512), BF16),
                 pltpu.VMEM((320, 768), BF16),
-                pltpu.VMEM((nz, 8, 512), F32),
+                pltpu.VMEM((nz, 16, 256), BF16),
                 pltpu.VMEM((2, 256, 256), F32),
                 pltpu.VMEM((192, 512), F32),
                 pltpu.VMEM((256, 256), F32),
                 pltpu.VMEM((4, 10, 8, 128), F32),
                 pltpu.VMEM((3, 10, 8, 128), F32),
-                pltpu.VMEM((2, 128, 256), BF16),
+                pltpu.VMEM((2, 2, 128, 512), BF16),
                 pltpu.VMEM((2, 256, 512), BF16),
                 pltpu.VMEM((2, 256, 512), BF16),
                 dma((8,)),

time: 37.5 us -> 34.6 us (0.923)
  Pallas kernels: 35.6 us -> 32.6 us
    pallas_call x1, Pallas kernels: 35.6 us -> 32.6 us  [per_device(): pl.pallas_call(kernel, out_shape=jax.ShapeDtypeStruct((16, 24, 256), F32)...]
where the time goes in v4:
time: 34.6 us; the launch traced here: 34.4 us
  Pallas kernels  32.6 us (94%)
  local copies, waits for them, and re-layouts  1.77 us (5%)
    pallas_call x1, Pallas kernels, per_device(): pl.pallas_call(kernel, out_shape=jax.ShapeDtypeStruct((16, 24, 256), F32)...  32.6 us
    unnamed x1, local copies, waits for them, and re-layouts  1.77 us

profile of v4, /device:TPU:1, one launch (start us, length us, event | category | flops | bytes accessed | tf_op | source)
XLA Modules:
  0.0 34.4 jit_solution(2791709817914827125)
XLA Ops:
  0.0 32.6 %shard_map.73 = f32[16,24,256]{2,1,0:T(8,128)} custom-call(bf16[16,24,256]{2,1,0:T(8,128)(2,1)} %q_hbm.1, bf16[9,9,9]{2,1,0:T(8,128)(2,1)} %kf_hbm.1, bf16[9,9,9]{2,1,0:T(8,128)(2,1)} %km_hbm.1, f32[8]{0:T(128)} %gw_hbm.1, f32[8]{0:T(128)} %gg_hbm.1, bf16[4,2560,768]{2,1,0:T(8,128)(2,1)} %constant.4.clone.cst_hbm, f32[4,32,512]{2,1,0:T(8,128)} %constant.5.clone.spread_hbm), custom_call_target="tpu_custom_call" | custom-call | tf_op jit(solution)/shard_map/pallas_call | solution.py:432
  32.6 1.8 %copy.9 = f32[16,24,256]{2,1,0:T(8,128)} copy(f32[16,24,256]{2,1,0:T(8,128)} %shard_map.73) | data formatting | bytes 786432

commit v5 on v4

--- a/solution.py
+++ b/solution.py
@@ -192,12 +192,14 @@
         copy.start()
     rest.start()
 
+    far_first = sorted(
+        range(1, nz), key=lambda d: -min(d // 8, 4 - d // 8) - min(d // 2 % 4, 4 - d // 2 % 4)
+    )
     barrier = pltpu.get_barrier_semaphore()
     for peer in ((ox, gy, gz), (gx, oy, gz), (ox, oy, gz), (gx, oy, up), (gx, oy, down)):
         pl.semaphore_signal(barrier, inc=1, device_id=peer, device_id_type=MESH)
 
-    @pl.loop(1, nz)
-    def _(d):
+    for d in far_first:
         pl.semaphore_signal(
             barrier, inc=1, device_id=(gx, gy, lax.rem(gz + d, nz)), device_id_type=MESH
         )
@@ -343,14 +345,7 @@
             total = term if total is None else total + term
         sfine[g] = total
 
-    for copy in two:
-        copy.wait_recv()
-    fm[0:6, :, 0:256] = fm[0:6, :, 0:256] * keep_low
-    fm[14:20, :, 0:256] = fm[14:20, :, 0:256] * keep_high
-    cross_m = send(fm.at[:, :, 0:256], fm.at[:, :, 256:512], s2, r2, 5, (ox, gy, gz))
-
-    @pl.loop(1, nz)
-    def _(d):
+    for d in far_first:
         gather(d, lax.rem(gz + nz - d, nz)).wait_recv()
 
     got = gath[...].reshape(512, 256)
@@ -378,6 +373,12 @@
     ways = [(oy + 2 * gx, (gx, oy, gz)), (oy + 2 * ox, (ox, oy, gz)), (gy + 2 * ox, (ox, gy, gz))]
     three = [send(dmat.at[w], rmat.at[i], s3, r3, i, peer) for i, (w, peer) in enumerate(ways)]
 
+    for copy in two:
+        copy.wait_recv()
+    fm[0:6, :, 0:256] = fm[0:6, :, 0:256] * keep_low
+    fm[14:20, :, 0:256] = fm[14:20, :, 0:256] * keep_high
+    cross_m = send(fm.at[:, :, 0:256], fm.at[:, :, 256:512], s2, r2, 5, (ox, gy, gz))
+
     cross_m.wait_recv()
     mpad[...] = dot(fm[...].reshape(320, 512), cst[2048:2560, :]).astype(BF16)
     for g in range(2):
@@ -398,6 +399,13 @@
     total = dot_t(back, high) + dot_t(back, low)
     total = total + sfine[...].reshape(16, 32, 256)[:, 0:24].reshape(384, 256)
     sfine_own = total
+
+    for copy in one + [cross_x] + two:
+        copy.wait_send()
+
+    @pl.loop(1, nz)
+    def _(d):
+        gather(d, gz).wait_send()
 
     for copy in three:
         copy.wait_recv()
@@ -414,12 +422,8 @@
     result = dot_t(up_high, high) + (dot_t(up_high, low) + dot_t(up_low, high)) + sfine_own
     out_ref[...] = result.reshape(16, 24, 256)
 
-    for copy in one + [cross_x] + two + [cross_m] + three:
+    for copy in [cross_m] + three:
         copy.wait_send()
-
-    @pl.loop(1, nz)
-    def _(d):
-        gather(d, gz).wait_send()
 
 
 def solution(mesh):

time: 34.6 us -> 32.1 us (0.928)
  Pallas kernels: 32.6 us -> 30.2 us
    pallas_call x1, Pallas kernels: 32.6 us -> 30.2 us  [per_device(): pl.pallas_call(kernel, out_shape=jax.ShapeDtypeStruct((16, 24, 256), F32)...]
where the time goes in v5:
time: 32.1 us; the launch traced here: 31.9 us
  Pallas kernels  30.2 us (94%)
  local copies, waits for them, and re-layouts  1.77 us (6%)
    pallas_call x1, Pallas kernels, per_device(): pl.pallas_call(kernel, out_shape=jax.ShapeDtypeStruct((16, 24, 256), F32)...  30.2 us
    unnamed x1, local copies, waits for them, and re-layouts  1.77 us

profile of v5, /device:TPU:1, one launch (start us, length us, event | category | flops | bytes accessed | tf_op | source)
XLA Modules:
  0.0 31.9 jit_solution(13407559127019052784)
XLA Ops:
  0.0 30.2 %shard_map.73 = f32[16,24,256]{2,1,0:T(8,128)} custom-call(bf16[16,24,256]{2,1,0:T(8,128)(2,1)} %q_hbm.1, bf16[9,9,9]{2,1,0:T(8,128)(2,1)} %kf_hbm.1, bf16[9,9,9]{2,1,0:T(8,128)(2,1)} %km_hbm.1, f32[8]{0:T(128)} %gw_hbm.1, f32[8]{0:T(128)} %gg_hbm.1, bf16[4,2560,768]{2,1,0:T(8,128)(2,1)} %constant.4.clone.cst_hbm, f32[4,32,512]{2,1,0:T(8,128)} %constant.5.clone.spread_hbm), custom_call_target="tpu_custom_call" | custom-call | tf_op jit(solution)/shard_map/pallas_call | solution.py:436
  30.2 1.8 %copy.9 = f32[16,24,256]{2,1,0:T(8,128)} copy(f32[16,24,256]{2,1,0:T(8,128)} %shard_map.73) | data formatting | bytes 786432

commit v6 on v5

--- a/solution.py
+++ b/solution.py
@@ -244,11 +244,15 @@
         return copy
 
     ways = [
-        (py.at[4:8], yz.at[0:4], (gx, oy, up)),
-        (py.at[0:4], yz.at[4:8], (gx, oy, down)),
-        (fq.at[16:20, :, 0:384], fq.at[0:4, :, 0:384], (gx, gy, up)),
-        (fq.at[4:8, :, 0:384], fq.at[20:24, :, 0:384], (gx, gy, down)),
+        (py.at[5:8], yz.at[1:4], (gx, oy, up)),
+        (py.at[0:2], yz.at[4:6], (gx, oy, down)),
+        (fq.at[17:20, :, 0:384], fq.at[1:4, :, 0:384], (gx, gy, up)),
+        (fq.at[4:6, :, 0:384], fq.at[20:22, :, 0:384], (gx, gy, down)),
         (py, yb, (gx, oy, gz)),
+        (py.at[4:5], yz.at[0:1], (gx, oy, up)),
+        (py.at[2:4], yz.at[6:8], (gx, oy, down)),
+        (fq.at[16:17, :, 0:384], fq.at[0:1, :, 0:384], (gx, gy, up)),
+        (fq.at[6:8, :, 0:384], fq.at[22:24, :, 0:384], (gx, gy, down)),
     ]
     one = [send(src, dst, s1, r1, i, peer) for i, (src, dst, peer) in enumerate(ways)]
 
@@ -280,28 +284,29 @@
         ezr[h, 0] = first_half
         ezr[h, 1] = second
 
-    for copy in one:
+    for copy in one[:5]:
         copy.wait_recv()
     keep_low = (gz > 0).astype(F32).astype(BF16)
     keep_high = (gz < nz - 1).astype(F32).astype(BF16)
-    fq[0:4, :, 0:384] = fq[0:4, :, 0:384] * keep_low
-    fq[20:24, :, 0:384] = fq[20:24, :, 0:384] * keep_high
     in_low = low_half.astype(F32).astype(BF16)
     in_high = jnp.logical_not(low_half).astype(F32).astype(BF16)
-    fq[0:4, :, 384:512] = yz[0:4] * in_high[0:4] * keep_low
+    fq[1:4, :, 0:384] = fq[1:4, :, 0:384] * keep_low
+    fq[20:22, :, 0:384] = fq[20:22, :, 0:384] * keep_high
+    fq[1:4, :, 384:512] = yz[1:4] * in_high[0:3] * keep_low
     fq[4:12, :, 384:512] = yb[...] * in_low
     fq[12:20, :, 384:512] = yb[...] * in_high
-    fq[20:24, :, 384:512] = yz[4:8] * in_low[0:4] * keep_high
-    known = fq[:, :, 0:512].reshape(384, 512)
-    px[...] = dot(known, cst[0:512, 0:256]).astype(BF16).reshape(24, 16, 256)
-    cross_x = send(px, fq.at[:, :, 512:768], s1, r1, 5, (ox, gy, gz))
+    fq[20:22, :, 384:512] = yz[4:6] * in_low[0:2] * keep_high
+    known = fq[1:22, :, 0:512].reshape(336, 512)
+    px[1:22] = dot(known, cst[0:512, 0:256]).astype(BF16).reshape(21, 16, 256)
+    cross_x = [send(px.at[1:22], fq.at[1:22, :, 512:768], s1, r1, 9, (ox, gy, gz))]
     plane_mid = dot(known, cst[512:1024, 0:128])
-    cross_x.wait_recv()
-    plane_mid = plane_mid + dot(fq[:, :, 512:768].reshape(384, 256), cst[1024:1280, 0:128])
-    rows = plane_mid.reshape(12, 2, 16, 128)
-    even, odd = rows[:, 0], rows[:, 1]
+    cross_x[0].wait_recv()
+    plane_mid = plane_mid + dot(fq[1:22, :, 512:768].reshape(336, 256), cst[1024:1280, 0:128])
+    rows = plane_mid.reshape(21, 16, 128)
+    rows = jnp.concatenate([rows, rows[0:1]], axis=0).reshape(11, 2, 16, 128)
+    odd, even = rows[:, 0], rows[:, 1]
     q_mid = (
-        even[2:10]
+        even[1:9]
         + (9.0 / 16.0) * (odd[1:9] + odd[2:10])
         + (-1.0 / 16.0) * (odd[0:8] + odd[3:11])
     ).astype(BF16)
@@ -337,6 +342,23 @@
     ]
     two = [send(src, dst, s2, r2, i, peer) for i, (src, dst, peer) in enumerate(ways)]
 
+    for copy in one[5:]:
+        copy.wait_recv()
+    for where, other, keep in (
+        (slice(0, 1), yz[0:1] * in_high[0:1], keep_low), (slice(22, 24), yz[6:8] * in_low[0:2], keep_high)
+    ):
+        count = where.stop - where.start
+        fq[where, :, 0:384] = fq[where, :, 0:384] * keep
+        fq[where, :, 384:512] = other * keep
+        px[where] = dot(fq[where, :, 0:512].reshape(16 * count, 512), cst[0:512, 0:256]).astype(
+            BF16
+        ).reshape(count, 16, 256)
+    cross_x += [
+        send(px.at[0:1], fq.at[0:1, :, 512:768], s1, r1, 10, (ox, gy, gz)),
+        send(px.at[22:24], fq.at[22:24, :, 512:768], s1, r1, 11, (ox, gy, gz)),
+    ]
+    for copy in cross_x[1:]:
+        copy.wait_recv()
     fpad[...] = dot(fq[...].reshape(384, 768), cst[1280:2048, :]).astype(BF16)
     for g in range(2):
         total = None
@@ -400,7 +422,7 @@
     total = total + sfine[...].reshape(16, 32, 256)[:, 0:24].reshape(384, 256)
     sfine_own = total
 
-    for copy in one + [cross_x] + two:
+    for copy in one + cross_x + two:
         copy.wait_send()
 
     @pl.loop(1, nz)
@@ -467,7 +489,7 @@
                 pltpu.VMEM((2, 256, 512), BF16),
                 pltpu.VMEM((2, 256, 512), BF16),
                 dma((8,)),
-                dma((6,)), dma((6,)),
+                dma((12,)), dma((12,)),
                 dma((6,)), dma((6,)),
                 dma((nz,)), dma((nz,)),
                 dma((3,)), dma((3,)),

time: 32.1 us -> 31.8 us (level)
  no operation moved by 1% of the time
where the time goes in v6:
time: 31.8 us; the launch traced here: 31.6 us
  Pallas kernels  29.9 us (94%)
  local copies, waits for them, and re-layouts  1.77 us (6%)
    pallas_call x1, Pallas kernels, per_device(): pl.pallas_call(kernel, out_shape=jax.ShapeDtypeStruct((16, 24, 256), F32)...  29.9 us
    unnamed x1, local copies, waits for them, and re-layouts  1.77 us

profile of v6, /device:TPU:1, one launch (start us, length us, event | category | flops | bytes accessed | tf_op | source)
XLA Modules:
  0.0 31.6 jit_solution(10515222035952148667)
XLA Ops:
  0.0 29.9 %shard_map.73 = f32[16,24,256]{2,1,0:T(8,128)} custom-call(bf16[16,24,256]{2,1,0:T(8,128)(2,1)} %q_hbm.1, bf16[9,9,9]{2,1,0:T(8,128)(2,1)} %kf_hbm.1, bf16[9,9,9]{2,1,0:T(8,128)(2,1)} %km_hbm.1, f32[8]{0:T(128)} %gw_hbm.1, f32[8]{0:T(128)} %gg_hbm.1, bf16[4,2560,768]{2,1,0:T(8,128)(2,1)} %constant.4.clone.cst_hbm, f32[4,32,512]{2,1,0:T(8,128)} %constant.5.clone.spread_hbm), custom_call_target="tpu_custom_call" | custom-call | tf_op jit(solution)/shard_map/pallas_call | solution.py:458
  29.9 1.8 %copy.9 = f32[16,24,256]{2,1,0:T(8,128)} copy(f32[16,24,256]{2,1,0:T(8,128)} %shard_map.73) | data formatting | bytes 786432

commit v7 on v6

--- a/solution.py
+++ b/solution.py
@@ -495,11 +495,16 @@
                 dma((3,)), dma((3,)),
             ],
             compiler_params=pltpu.CompilerParams(
-                collective_id=0, has_side_effects=True, vmem_limit_bytes=63 * 2**20
+                collective_id=0, has_side_effects=True, vmem_limit_bytes=40 * 2**20
             ),
         )(
-            charges, kernel_fine, kernel_mid, gauss_width, gauss_weight,
-            jnp.asarray(whole), jnp.asarray(spread),
+            *[
+                pltpu.with_memory_space_constraint(a, pltpu.HBM)
+                for a in (
+                    charges, kernel_fine, kernel_mid, gauss_width, gauss_weight,
+                    jnp.asarray(whole), jnp.asarray(spread),
+                )
+            ]
         )
 
     placed = (P("gx", "gy", "gz"), P(), P(), P(), P())

time: 31.8 us -> 30 us (0.943)
  local copies, waits for them, and re-layouts: 1.77 us -> 0.75 us
  Pallas kernels: 29.9 us -> 29.1 us
    unnamed x1, local copies, waits for them, and re-layouts: 1.77 us -> 0.75 us
    pallas_call x1, Pallas kernels: 29.9 us -> 29.1 us  [per_device(): pl.pallas_call(kernel, out_shape=jax.ShapeDtypeStruct((16, 24, 256), F32)...]
where the time goes in v7:
time: 30 us; the launch traced here: 29.9 us
  Pallas kernels  29.1 us (97%)
  local copies, waits for them, and re-layouts  0.75 us (2%)
    pallas_call x1, Pallas kernels, per_device(): pl.pallas_call(kernel, out_shape=jax.ShapeDtypeStruct((16, 24, 256), F32)...  29.1 us
    unnamed x1, local copies, waits for them, and re-layouts  0.75 us

profile of v7, /device:TPU:1, one launch (start us, length us, event | category | flops | bytes accessed | tf_op | source)
XLA Modules:
  0.0 29.9 jit_solution(8817542562563885768)
XLA Ops:
  0.0 29.1 %shard_map.73 = f32[16,24,256]{2,1,0:T(8,128)S(1)} custom-call(bf16[16,24,256]{2,1,0:T(8,128)(2,1)} %q_hbm.1, bf16[9,9,9]{2,1,0:T(8,128)(2,1)} %kf_hbm.1, bf16[9,9,9]{2,1,0:T(8,128)(2,1)} %km_hbm.1, f32[8]{0:T(128)} %gw_hbm.1, f32[8]{0:T(128)} %gg_hbm.1, bf16[4,2560,768]{2,1,0:T(8,128)(2,1)} %constant.4.clone.cst_hbm, f32[4,32,512]{2,1,0:T(8,128)} %constant.5.clone.spread_hbm), custom_call_target="tpu_custom_call" | custom-call | tf_op jit(solution)/shard_map/pallas_call | solution.py:458
  29.1 0.7 %copy.9 = f32[16,24,256]{2,1,0:T(8,128)} copy(f32[16,24,256]{2,1,0:T(8,128)S(1)} %shard_map.73) | data formatting | bytes 786432

commit v8 on v7

--- a/solution.py
+++ b/solution.py
@@ -334,9 +334,9 @@
         gather(d, gz).start()
 
     ways = [
-        (fm.at[8:14, :, 0:128], fm.at[0:6, :, 128:256], (gx, oy, up)),
+        (fm.at[9:14, :, 0:128], fm.at[1:6, :, 128:256], (gx, oy, up)),
         (fm.at[6:12, :, 0:128], fm.at[14:20, :, 128:256], (gx, oy, down)),
-        (fm.at[8:14, :, 0:128], fm.at[0:6, :, 0:128], (gx, gy, up)),
+        (fm.at[9:14, :, 0:128], fm.at[1:6, :, 0:128], (gx, gy, up)),
         (fm.at[6:12, :, 0:128], fm.at[14:20, :, 0:128], (gx, gy, down)),
         (fm.at[6:14, :, 0:128], fm.at[6:14, :, 128:256], (gx, oy, gz)),
     ]
@@ -391,13 +391,14 @@
     share = share + (dot(high[0:128], wlo[1]) + dot(high[128:256], whi[1]))
     share = jnp.swapaxes(share.reshape(8, 16, 512), 0, 1)
     for w in range(4):
-        dmat[w] = share[0:10, :, 128 * w : 128 * w + 128]
+        dmat[w] = share[1:10, :, 128 * w : 128 * w + 128]
     ways = [(oy + 2 * gx, (gx, oy, gz)), (oy + 2 * ox, (ox, oy, gz)), (gy + 2 * ox, (ox, gy, gz))]
     three = [send(dmat.at[w], rmat.at[i], s3, r3, i, peer) for i, (w, peer) in enumerate(ways)]
 
     for copy in two:
         copy.wait_recv()
-    fm[0:6, :, 0:256] = fm[0:6, :, 0:256] * keep_low
+    fm[0:1, :, 0:256] = jnp.zeros((1, 16, 256), BF16)
+    fm[1:6, :, 0:256] = fm[1:6, :, 0:256] * keep_low
     fm[14:20, :, 0:256] = fm[14:20, :, 0:256] * keep_high
     cross_m = send(fm.at[:, :, 0:256], fm.at[:, :, 256:512], s2, r2, 5, (ox, gy, gz))
 
@@ -432,7 +433,7 @@
     for copy in three:
         copy.wait_recv()
     top = (dmat[variant] + rmat[2]) + (rmat[0] + rmat[1])
-    mid = interleave(top[2:8], widen(top[1:10], 6))
+    mid = interleave(top[1:7], widen(top, 6))
     mid = trimmed(mid)
     fine = interleave(mid[2:10], widen(mid[1:12], 8))
     lower = lax.broadcasted_iota(jnp.int32, (16, 8, 128), 2) < 64
@@ -483,8 +484,8 @@
                 pltpu.VMEM((2, 256, 256), F32),
                 pltpu.VMEM((192, 512), F32),
                 pltpu.VMEM((256, 256), F32),
-                pltpu.VMEM((4, 10, 8, 128), F32),
-                pltpu.VMEM((3, 10, 8, 128), F32),
+                pltpu.VMEM((4, 9, 8, 128), F32),
+                pltpu.VMEM((3, 9, 8, 128), F32),
                 pltpu.VMEM((2, 2, 128, 512), BF16),
                 pltpu.VMEM((2, 256, 512), BF16),
                 pltpu.VMEM((2, 256, 512), BF16),

time: 30 us -> 29.9 us (level)
  no operation moved by 1% of the time
where the time goes in v8:
time: 29.9 us; the launch traced here: 29.8 us
  Pallas kernels  29 us (97%)
  local copies, waits for them, and re-layouts  0.75 us (3%)
    pallas_call x1, Pallas kernels, per_device(): pl.pallas_call(kernel, out_shape=jax.ShapeDtypeStruct((16, 24, 256), F32)...  29 us
    unnamed x1, local copies, waits for them, and re-layouts  0.75 us

profile of v8, /device:TPU:1, one launch (start us, length us, event | category | flops | bytes accessed | tf_op | source)
XLA Modules:
  0.0 29.8 jit_solution(5661374041204401000)
XLA Ops:
  0.0 29.0 %shard_map.73 = f32[16,24,256]{2,1,0:T(8,128)S(1)} custom-call(bf16[16,24,256]{2,1,0:T(8,128)(2,1)} %q_hbm.1, bf16[9,9,9]{2,1,0:T(8,128)(2,1)} %kf_hbm.1, bf16[9,9,9]{2,1,0:T(8,128)(2,1)} %km_hbm.1, f32[8]{0:T(128)} %gw_hbm.1, f32[8]{0:T(128)} %gg_hbm.1, bf16[4,2560,768]{2,1,0:T(8,128)(2,1)} %constant.4.clone.cst_hbm, f32[4,32,512]{2,1,0:T(8,128)} %constant.5.clone.spread_hbm), custom_call_target="tpu_custom_call" | custom-call | tf_op jit(solution)/shard_map/pallas_call | solution.py:459
  29.0 0.7 %copy.9 = f32[16,24,256]{2,1,0:T(8,128)} copy(f32[16,24,256]{2,1,0:T(8,128)S(1)} %shard_map.73) | data formatting | bytes 786432
